TPU v7x, 256 devices: a whole 4x4x8 slice. The times are simulated.
256 devices in a mesh: expert: 64 (over z, x, y_hi), etp: 4 (over y_lo, core).
Axes of the slice: x: 4, y: 4 (y_hi: 2, y_lo: 2; y = y_hi * 2 + y_lo), z: 8, core: 2. Of those that a mesh axis runs over, the one named last changes fastest.
Arguments:
- hidden_act: bfloat16 [64, 1024, 2880], P('expert', None, 'etp'), may hold values from -6 to 6
- down_weight: bfloat16 [64, 2880, 2880], P('expert', 'etp'), may hold values from -0.109375 to 0.109375
- out_grad: bfloat16 [8192, 2880], P('expert', 'etp'), may hold values from -1.5 to 1.5
- route_probs: float32 [8192, 4], P('expert'), may hold values from 0.05 to 1
- expert_ids: int32 [8192, 4], P('expert'), may hold values from 0 to 63, all different within a row; in each aligned block of 128 rows (0 to 127, 128 to 255, ...) at most 16 rows name the same one
Outputs:
- weight_grad: bfloat16 [64, 2880, 2880], P('expert', 'etp')
- hidden_grad: bfloat16 [64, 1024, 2880], P('expert', None, 'etp')
- prob_grad: float32 [8192, 4], P('expert')
Inputs may be any that keep to these rules, and one draw needn't show every extreme that they name: `expert_ids`: each token names 4 different experts; among the 128 tokens held by one device index along the mesh axis `expert` no expert is named more than 16 times, a bound that some block reaches.
All inputs are finite; a program needn't handle non-finite values.
Results may differ from a plain program's by a relative error of at most 0.015.
Values may be sent and summed in bfloat16 or wider, within the bound.
A program may use at most 128 MiB of HBM per device.

v0:
```python
import jax
import jax.numpy as jnp
from jax import lax
from jax.experimental import pallas as pl
from jax.experimental.pallas import tpu as pltpu
from jax.sharding import PartitionSpec as P

BF = jnp.bfloat16
F32 = jnp.float32
MESH = pl.DeviceIdType.MESH

TOKENS = 128
TOP = 4
QUARTER = 720
WIDTH = 2880
CHUNK = 768
HALF = 384
META = 2 * CHUNK + 2 * CHUNK - 256
SLOT = 16
PLANES = 8
COLS = 4
PLANE = 8

SCHEDULE = (
    "A00", "A01", "M0", "A10", "A20", "C00", "C01", "M1", "A11", "A21", "M2", "C10",
    "C20", "A30", "A40", "C11", "C21", "M3", "A31", "A41", "D00", "D01", "C30", "C40",
    "M4", "A50", "A60", "C31", "C41", "A51", "A61", "M5", "D10", "D11", "C50", "C60",
    "A70", "A71", "C51", "C61", "G0", "C70", "C71", "K0", "K1", "K2", "D20", "D21",
    "D30", "D31", "G1", "K3", "K4", "K5", "K6", "K7", "D40", "D41", "D50", "D51",
    "G2", "D60", "D61", "D70", "D71", "G3",
)


def dot(a, b, ca, cb):
    return lax.dot_general(a, b, (((ca,), (cb,)), ((), ())), preferred_element_type=F32)


def iota(shape, dim):
    return lax.broadcasted_iota(jnp.int32, shape, dim)


def onehot(cond):
    return jnp.where(cond, 1.0, 0.0).astype(BF)


def keep(a0, a1, a2, a3):
    b01, b02, b03 = a0 >= a1, a0 >= a2, a0 >= a3
    b12, b13, b23 = a1 >= a2, a1 >= a3, a2 >= a3
    n01, n02, n03 = ~b01, ~b02, ~b03
    n12, n13, n23 = ~b12, ~b13, ~b23

    def two(a, b, c):
        return onehot((a & b) | (c & (a | b)))

    return two(b01, b02, b03), two(n01, b12, b13), two(n02, n12, b23), two(n03, n13, n23)


def kernel(
    ids_ref, probs_ref, og_ref, w_hbm, hid_hbm,
    wg_ref, hg_ref, pg_ref,
    nb, zb0, zb1, selb, dsel, fwd, bwd, up, down, rows, wv, wc, wr, rm, acc, hid, hsb, kmask, sc, etp_in, pln_in, zout, zin,
    nb_s, nb_r, z_s, z_r, p_s, p_r, l_s, y_s, y_r, s_s, s_r,
    r1_s, r1_r, r2_s, r2_r, r3_s, r3_r, w_sem, hid_sem,
):
    e = lax.axis_index("expert")
    q = lax.axis_index("etp")
    z = e // PLANE
    x = (e // 2) % COLS
    yh = e % 2
    ylo, core = q // 2, q % 2
    q1 = ylo * 2 + 1 - core
    q2 = (1 - ylo) * 2 + core
    q3 = (1 - ylo) * 2 + 1 - core
    pending = []

    def send(src, dst, ss, rs, dev):
        cp = pltpu.make_async_remote_copy(src, dst, ss, rs, device_id=dev, device_id_type=MESH)
        cp.start()
        pending.append(cp)

    def arrived(ref, sem):
        pltpu.make_async_copy(ref, ref, sem).wait()

    def zdev(d):
        return (((z + d) % PLANES) * PLANE + e % PLANE, q)

    def rel(i):
        return -((i + 1) // 2) if i % 2 else i // 2

    rels = [(dx, dy) for dy in range(2) for dx in range(COLS) if (dx, dy) != (0, 0)]

    def plane_to(dx, dy):
        ex = z * PLANE + ((x + dx) % COLS) * 2 + (yh if dy == 0 else 1 - yh)
        return (ex, q if dy == 0 else q2)

    w_cp = pltpu.make_async_copy(w_hbm, wv, w_sem)
    w_cp.start()
    hid_cp = []
    for i in range(PLANES):
        src = (z + rel(i) + PLANES) % PLANES
        cp = pltpu.make_async_copy(
            hid_hbm.at[:, pl.ds(pl.multiple_of(src * 128, 128), 128)],
            hid.at[:, pl.ds(i * 128, 128)], hid_sem.at[i])
        cp.start()
        hid_cp.append(cp)

    peers = [zdev(d) for d in range(1, PLANES)]
    peers += [plane_to(dx, dy) for dx, dy in rels]
    peers += [(e, (q + d) % 4) for d in range(1, 4)]
    barrier = pltpu.get_barrier_semaphore()
    for dev in peers:
        pl.semaphore_signal(barrier, inc=1, device_id=dev, device_id_type=MESH)
    lane = iota((128, 128), 1)
    sub = iota((128, 128), 0)
    eye = lane == sub
    before = onehot(sub < lane)
    sub_expert = (sub // SLOT).astype(F32)
    sub_rank = (sub % SLOT).astype(F32)

    def column(r):
        return jnp.sum(jnp.where(eye, r, 0.0), axis=1, keepdims=True)

    def as_row(c):
        return jnp.sum(jnp.where(eye, c, 0.0), axis=0, keepdims=True)

    def routes(ids, plane):
        ex = sub_expert + (plane * PLANE).astype(F32)
        eqs = [ids[k:k + 1, :] == ex for k in range(TOP)]
        any_k = eqs[0] | eqs[1] | eqs[2] | eqs[3]
        rank = dot(onehot(any_k), before, 1, 0)
        return eqs, any_k, rank == sub_rank

    ids_f = ids_ref[...].astype(F32)
    diff = iota((QUARTER, HALF), 0) - iota((QUARTER, HALF), 1)
    zb0[0, 0:128, :] = dot(og_ref[...], onehot(diff == 48 * q), 0, 0).astype(BF)
    zb0[0, 128:144, 0:128] = jnp.concatenate([ids_f, jnp.zeros((12, 128), F32)], axis=0).astype(BF)
    zb0[0, 128:144, 128:HALF] = jnp.zeros((16, HALF - 128), BF)
    pl.semaphore_wait(barrier, len(peers))

    def zsend(src, i, h, d):
        buf = zb1 if h else zb0
        send(buf.at[src], buf.at[i], z_s.at[i, h], z_r.at[i, h], zdev(d % PLANES))

    send(og_ref.at[pl.ds(0, 144), :], nb, nb_s, nb_r, (e, (q + 3) % 4))
    zsend(0, 1, 0, 1)
    zsend(0, 2, 0, -1)

    probs = probs_ref[...]
    own_ids = [column(ids_f[k:k + 1, :]) for k in range(TOP)]
    own_probs = [column(probs[k:k + 1, :]) for k in range(TOP)]

    def meta(off):
        out = jnp.zeros((128, 128), F32)
        for k in range(TOP):
            hi = own_probs[k].astype(BF).astype(F32)
            rest = own_probs[k] - hi
            mid = rest.astype(BF).astype(F32)
            lo = rest - mid
            for part, v in enumerate((own_ids[k], hi, mid, lo)):
                out = out + jnp.where(lane == off + 4 * part + k, v, 0.0)
        return out

    def step_second():
        chunk = dot(og_ref[...], onehot(diff == 48 * q + HALF), 0, 0)
        last = jnp.where(q == 3, 1.0, 0.0)
        tile = last * meta(64)
        arrived(nb, nb_r)
        gap = jnp.where(q < 3, 48 * q - QUARTER + HALF, 100000)
        chunk = chunk + dot(nb[...], onehot(diff[:144] == gap), 0, 0)
        zb1[0] = chunk.astype(BF)
        zb1[0, :, 128:256] = (chunk[:, 128:256] + tile).astype(BF)
        zsend(0, 1, 1, 1)
        zsend(0, 2, 1, -1)

    def lanes_of(qq, h):
        return pl.ds(pl.multiple_of(qq * CHUNK + h * HALF, 128), HALF)

    def step_a(i, h):
        buf = zb1 if h else zb0
        if i == 0 and h == 1:
            step_second()
        if i > 0:
            arrived(buf.at[i], z_r.at[i, h])
            if i in (1, 3) or (i, h) == (5, 0):
                zsend(i, i + 2, h, 1)
            if i in (2, 4):
                zsend(i, i + 2, h, -1)
            if (i, h) == (6, 1):
                zsend(i, 7, h, -1)
        if h == 0:
            _, any_k, hit = routes(zb0[i, 128:144, 0:128].astype(F32), z)
            dsel[i] = onehot(any_k & hit)
        picked = dot(dsel[i], buf[i, 0:128, :], 1, 0)
        selb[i, h] = picked.astype(BF).reshape(COLS, 2, SLOT, HALF)
        for dx, dy in rels:
            xt = (x + dx) % COLS
            yt = yh if dy == 0 else 1 - yh
            at = dy * COLS + dx
            send(selb.at[i, h, xt, yt], rows.at[i, x, yh, :, lanes_of(q, h)],
                 p_s.at[i, h, at], p_r.at[i, h, at], plane_to(dx, dy))
        pltpu.make_async_copy(
            selb.at[i, h, x, yh], rows.at[i, x, yh, :, lanes_of(q, h)], l_s.at[i, h]).start()

    def half(i, y, qq, h):
        return rows.at[i, :, y, :, lanes_of(qq, h)]

    def step_c(i, h):
        arrived(selb.at[i, h, 0, 0], l_s.at[i, h])
        for dx, dy in rels:
            xs = (x - dx + COLS) % COLS
            ys = yh if dy == 0 else 1 - yh
            qs = q if dy == 0 else q2
            arrived(rows.at[i, xs, ys, :, lanes_of(qs, h)], p_r.at[i, h, dy * COLS + dx])
        one, two = half(i, yh, q, h), half(i, 1 - yh, q2, h)
        send(one, one, y_s.at[i, h, 0], y_r.at[i, h, 0], (e, q2))
        send(two, two, y_s.at[i, h, 1], y_r.at[i, h, 1], (e, q2))
        send(one, one, s_s.at[i, h, 0], s_r.at[i, h, 0], (e, q1))
        send(two, two, s_s.at[i, h, 1], s_r.at[i, h, 1], (e, q1))

    def step_d(i, h):
        one, two = half(i, yh, q2, h), half(i, 1 - yh, q, h)
        arrived(one, y_r.at[i, h, 0])
        send(one, one, s_s.at[i, h, 2], s_r.at[i, h, 2], (e, q1))
        arrived(two, y_r.at[i, h, 1])
        send(two, two, s_s.at[i, h, 3], s_r.at[i, h, 3], (e, q1))

    def tables():
        f, c = iota((512, 512), 0), iota((512, 512), 1)
        fwd[...] = onehot((c % 128 == f // 4) & (c // 128 == f % 4))
        c, f = iota((512, 512), 0), iota((512, 512), 1)
        bwd[...] = onehot((c % 128 == f // 4) & (c // 128 == f % 4))
        c, f = iota((256, 240), 0), iota((256, 240), 1)
        up[...] = onehot((c % 64 == f // 4) & (c // 64 == f % 4))
        f, c = iota((240, 256), 0), iota((240, 256), 1)
        down[...] = onehot((c % 64 == f // 4) & (c // 64 == f % 4))

    def step_m(b):
        if b == 0:
            tables()
            w_cp.wait()
        lo = 512 * b
        n = min(512, WIDTH - lo)
        wb = wv[:, lo:lo + n]
        a = jnp.abs(dot(wb, fwd[0:n, :], 1, 0)).astype(BF)
        kept = jnp.concatenate(keep(*[a[:, 128 * p:128 * p + 128] for p in range(4)]), axis=1)
        wc[:, lo:lo + n] = wb * dot(kept, bwd[:, 0:n], 1, 0).astype(BF)
        for m in range(3):
            part = wb[240 * m:240 * m + 240]
            a = jnp.abs(dot(up[...], part, 1, 0)).astype(BF)
            kept = jnp.concatenate(keep(*[a[64 * p:64 * p + 64] for p in range(4)]), axis=0)
            mask = dot(down[...], kept, 1, 0).astype(BF)
            rm[240 * m:240 * m + 240, lo:lo + n] = mask
            wr[240 * m:240 * m + 240, lo:lo + n] = part * mask

    def step_k(i):
        eqs, _, hit = routes(ids_f, (z - rel(i) + PLANES) % PLANES)
        for k in range(TOP):
            kmask[i, k] = jnp.where(eqs[k] & hit, 1.0, 0.0)

    def step_g(g):
        for i in (2 * g, 2 * g + 1):
            for h in range(2):
                arrived(half(i, yh, q1, h), s_r.at[i, h, 0])
                arrived(half(i, 1 - yh, q3, h), s_r.at[i, h, 1])
                arrived(half(i, yh, q3, h), s_r.at[i, h, 2])
                arrived(half(i, 1 - yh, q1, h), s_r.at[i, h, 3])
            hid_cp[i].wait()
        span = pl.ds(256 * g, 256)

        def r(lo, n):
            return rows[2 * g:2 * g + 2, :, :, :, lo:lo + n].reshape(256, n)

        back = dot(wr[...], r(0, WIDTH), 1, 1)
        score = jnp.sum(hid[:, span].astype(F32) * back, axis=0, keepdims=True)
        sc[2 * g:2 * g + 1, :] = score[:, :128]
        sc[2 * g + 1:2 * g + 2, :] = score[:, 128:]
        if g == 3:
            return_one()
        mt = r(META, 128).astype(F32)
        total = pltpu.roll(mt, 124, 1) + pltpu.roll(mt, 120, 1) + pltpu.roll(mt, 116, 1)
        wide = iota((256, 128), 1)
        mine = (wide >= 64) & (wide < 68) & (mt == e.astype(F32))
        pc = jnp.sum(jnp.where(mine, total, 0.0), axis=1, keepdims=True)
        pr = jnp.concatenate([as_row(pc[:128]), as_row(pc[128:])], axis=1)
        grad = (dot(wc[...], r(0, WIDTH), 1, 1) * pr).astype(BF)
        for i in (2 * g, 2 * g + 1):
            src = (z + rel(i) + PLANES) % PLANES
            part = 128 * (i % 2)
            hg_ref[:, pl.ds(pl.multiple_of(src * 128, 128), 128)] = grad[:, part:part + 128]
        hsb[...] = (hid[:, span].astype(F32) * pr).astype(BF)
        if g == 3:
            return_two()
        if g < 3:
            for c in range(4):
                n = min(CHUNK, WIDTH - CHUNK * c)
                part = dot(hsb[...], r(CHUNK * c, n), 1, 0)
                if g > 0:
                    part = part + acc[:, CHUNK * c:CHUNK * c + n]
                acc[:, CHUNK * c:CHUNK * c + n] = part
        else:
            for m in range(3):
                at = slice(240 * m, 240 * m + 240)
                for c in range(4):
                    n = min(CHUNK, WIDTH - CHUNK * c)
                    ln = slice(CHUNK * c, CHUNK * c + n)
                    part = dot(hsb[at, :], r(CHUNK * c, n), 1, 0) + acc[at, ln]
                    wg_ref[at, ln] = jnp.where(rm[at, ln].astype(F32) > 0.5, part, 0.0).astype(BF)
                if m == 0:
                    return_three()

    def return_one():
        etp_in[q] = sc[...]
        for d in range(1, 4):
            send(etp_in.at[q], etp_in.at[q], r1_s.at[d], r1_r.at[d], (e, (q + d) % 4))

    def return_two():
        for d in range(1, 4):
            arrived(etp_in.at[(q - d + 4) % 4], r1_r.at[d])
        sc[...] = (etp_in[0] + etp_in[1]) + (etp_in[2] + etp_in[3])
        for dx, dy in rels:
            send(sc, pln_in.at[dy * COLS + dx], r2_s.at[dy * COLS + dx],
                 r2_r.at[dy * COLS + dx], plane_to(dx, dy))

    def return_three():
        lane8 = iota((8, 128), 1) // SLOT
        own = 2 * x + yh
        v = jnp.where(lane8 == own, sc[...], 0.0)
        for dx, dy in rels:
            arrived(pln_in.at[dy * COLS + dx], r2_r.at[dy * COLS + dx])
            sb = 2 * ((x - dx + COLS) % COLS) + (yh if dy == 0 else 1 - yh)
            shifted = pltpu.roll(pln_in[dy * COLS + dx], ((sb - own + PLANE) % PLANE) * SLOT, 1)
            v = v + jnp.where(lane8 == sb, shifted, 0.0)
        zout[...] = v
        for i in range(1, PLANES):
            send(zout, zin.at[i], r3_s.at[i], r3_r.at[i], zdev((rel(i) + PLANES) % PLANES))

    def return_four():
        totals = [jnp.zeros((128, 128), F32) for _ in range(TOP)]
        for i in range(PLANES):
            if i == 0:
                v = column(zout[0:1, :])
            else:
                arrived(zin.at[i], r3_r.at[i])
                v = column(zin[i, i:i + 1, :])
            for k in range(TOP):
                totals[k] = totals[k] + kmask[i, k] * v
        for k in range(TOP):
            pg_ref[k:k + 1, :] = jnp.sum(totals[k], axis=0, keepdims=True)

    steps = {"A": step_a, "C": step_c, "D": step_d, "M": step_m, "K": step_k, "G": step_g}
    for item in SCHEDULE:
        steps[item[0]](*[int(c) for c in item[1:]])
    return_four()
    for cp in pending:
        cp.wait_send()


def call(ids, probs, og, weight, hidden):
    hbm = pl.BlockSpec(memory_space=pltpu.HBM)
    out = pl.BlockSpec(memory_space=pltpu.VMEM)
    vmem = pl.BlockSpec(memory_space=pltpu.VMEM)
    dma = pltpu.SemaphoreType.DMA
    return pl.pallas_call(
        kernel,
        out_shape=(
            pltpu.VMEM((QUARTER, WIDTH), BF),
            pltpu.VMEM((QUARTER, 1024), BF),
            jax.ShapeDtypeStruct((TOP, TOKENS), F32),
        ),
        in_specs=[vmem, vmem, vmem, hbm, hbm],
        out_specs=(out, out, vmem),
        scratch_shapes=[
            pltpu.VMEM((144, TOKENS), BF),
            pltpu.VMEM((8, TOKENS + 16, HALF), BF),
            pltpu.VMEM((8, TOKENS, HALF), BF),
            pltpu.VMEM((8, 2, COLS, 2, SLOT, HALF), BF),
            pltpu.VMEM((8, 128, 128), BF),
            pltpu.VMEM((512, 512), BF),
            pltpu.VMEM((512, 512), BF),
            pltpu.VMEM((256, 240), BF),
            pltpu.VMEM((240, 256), BF),
            pltpu.VMEM((8, COLS, 2, SLOT, 4 * CHUNK), BF),
            pltpu.VMEM((QUARTER, WIDTH), BF),
            pltpu.VMEM((QUARTER, WIDTH), BF),
            pltpu.VMEM((QUARTER, WIDTH), BF),
            pltpu.VMEM((QUARTER, WIDTH), BF),
            pltpu.VMEM((QUARTER, WIDTH), F32),
            pltpu.VMEM((QUARTER, 1024), BF),
                pltpu.VMEM((QUARTER, 256), BF),
            pltpu.VMEM((8, TOP, 128, 128), F32),
            pltpu.VMEM((8, 128), F32),
            pltpu.VMEM((4, 8, 128), F32),
            pltpu.VMEM((8, 8, 128), F32),
            pltpu.VMEM((8, 128), F32),
            pltpu.VMEM((8, 8, 128), F32),
            dma, dma, dma((8, 2)), dma((8, 2)), dma((8, 2, 8)), dma((8, 2, 8)), dma((8, 2)),
            dma((8, 2, 2)), dma((8, 2, 2)), dma((8, 2, 4)), dma((8, 2, 4)),
            dma((4,)), dma((4,)), dma((8,)), dma((8,)), dma((8,)), dma((8,)),
            dma, dma((8,)),
        ],
        compiler_params=pltpu.CompilerParams(
            collective_id=0, has_side_effects=True, vmem_limit_bytes=50 * 1024 * 1024),
        cost_estimate=pl.CostEstimate(
            flops=3 * 2 * 1024 * 720 * 2880, bytes_accessed=20_000_000, transcendentals=0),
    )(ids, probs, og, weight, hidden)


def local(hidden_act, down_weight, out_grad, route_probs, expert_ids):
    wg, hg, pg = call(
        expert_ids.T, route_probs.T, out_grad.T, down_weight[0], hidden_act[0].T)
    return wg[None], hg.T[None], pg.T


def solution(mesh):
    return jax.shard_map(
        local,
        mesh=mesh,
        in_specs=(
            P("expert", None, "etp"),
            P("expert", "etp", None),
            P("expert", "etp"),
            P("expert", None),
            P("expert", None),
        ),
        out_specs=(P("expert", "etp", None), P("expert", None, "etp"), P("expert", None)),
        check_vma=False,
    )
```

profile of v0, /device:TPU:1, one launch (start us, length us, event | category | flops | bytes accessed | tf_op | source)
XLA Modules:
  0.0 80.6 jit_solution(3219211174971338760)
XLA Ops:
  0.6 76.3 %shard_map.76 = (bf16[720,2880]{1,0:T(8,128)(2,1)S(1)}, bf16[720,1024]{1,0:T(8,128)(2,1)S(1)}, f32[4,128]{1,0:T(4,128)}) custom-call(s32[4,128]{1,0:T(4,128)} %bitcast.18, f32[4,128]{1,0:T(4,128)} %bitcast.19, bf16[720,128]{1,0:T(8,128)(2,1)} %bitcast.17, bf16[720,2880]{1,0:T(8,128)(2,1)} %bitcast.15, bf16[720,1024]{1,0:T(8,128)(2,1)} %bitcast.16), custom_call_target="tpu_custom_call" | custom-call | flops 12740198400 | bytes 20000000 | tf_op jit(solution)/shard_map/pallas_call | solution.py:363
  76.9 0.0 copy-start
  76.9 2.0 %copy.11 = bf16[1,720,2880]{2,1,0:T(8,128)(2,1)} copy(bf16[1,720,2880]{2,1,0:T(8,128)(2,1)S(1)} %bitcast.12) | data formatting | bytes 8294400
  78.9 1.1 %copy.12 = bf16[1,1024,720]{1,2,0:T(8,128)(2,1)} copy(bf16[1,1024,720]{1,2,0:T(8,128)(2,1)S(1)} %bitcast.13) | data formatting | bytes 2949120
  80.1 0.0 copy-done
  80.1 0.6 copy.13
Async XLA Ops:
  76.9 3.2 %copy-start = (f32[4,128]{1,0:T(4,128)S(1)}, f32[4,128]{1,0:T(4,128)}, u32[]{:S(2)}) copy-start(f32[4,128]{1,0:T(4,128)} %get-tuple-element.8) | copy-start | bytes 6148
where the time goes:
time: 80.7 us; the launch traced here: 80.6 us
  Pallas kernels  76.3 us (95%)
  local copies, waits for them, and re-layouts  3.72 us (5%)
    pallas_call x1, Pallas kernels, call(): pl.pallas_call(kernel, out_shape=(pltpu.VMEM((QUARTER, WIDTH), BF), pltpu...  76.3 us
    unnamed x5, local copies, waits for them, and re-layouts  3.72 us

commit v1 on v0

--- a/solution.py
+++ b/solution.py
@@ -14,7 +14,8 @@
 QUARTER = 720
 WIDTH = 2880
 CHUNK = 768
-HALF = 384
+LATE = 512
+EARLY = 256
 META = 2 * CHUNK + 2 * CHUNK - 256
 SLOT = 16
 PLANES = 8
@@ -22,12 +23,14 @@
 PLANE = 8
 
 SCHEDULE = (
-    "A00", "A01", "M0", "A10", "A20", "C00", "C01", "M1", "A11", "A21", "M2", "C10",
-    "C20", "A30", "A40", "C11", "C21", "M3", "A31", "A41", "D00", "D01", "C30", "C40",
-    "M4", "A50", "A60", "C31", "C41", "A51", "A61", "M5", "D10", "D11", "C50", "C60",
-    "A70", "A71", "C51", "C61", "G0", "C70", "C71", "K0", "K1", "K2", "D20", "D21",
-    "D30", "D31", "G1", "K3", "K4", "K5", "K6", "K7", "D40", "D41", "D50", "D51",
-    "G2", "D60", "D61", "D70", "D71", "G3",
+    "A00", "M0", "A01", "A02", "C00", "A10", "A20", "M1", "C01", "C02", "A11", "A21",
+    "A12", "A22", "C10", "C20", "M2", "A30", "A40", "C11", "C21", "C12", "C22", "A31",
+    "A41", "A32", "A42", "D0", "M3", "C30", "C40", "A50", "A60", "C31", "C41", "C32",
+    "C42", "A51", "A61", "A52", "A62", "D1", "M4", "C50", "C60", "A70", "A71", "A72",
+    "C51", "C61", "C52", "C62", "M5", "C70", "C71", "C72", "D2", "K0", "K1", "K2",
+    "K3", "B0", "W0", "D3", "D4", "B1", "W1", "K4", "K5", "K6", "K7", "D5",
+    "D6", "B2", "D7", "B3", "R1", "W2", "H1", "R2", "W3", "H2", "R3", "H3",
+    "H0", "R4",
 )
 
 
@@ -58,8 +61,8 @@
 def kernel(
     ids_ref, probs_ref, og_ref, w_hbm, hid_hbm,
     wg_ref, hg_ref, pg_ref,
-    nb, zb0, zb1, selb, dsel, fwd, bwd, up, down, rows, wv, wc, wr, rm, acc, hid, hsb, kmask, sc, etp_in, pln_in, zout, zin,
-    nb_s, nb_r, z_s, z_r, p_s, p_r, l_s, y_s, y_r, s_s, s_r,
+    nb, zb0, zb1, zb2, sb0, sb1, sb2, dsel, fwd, bwd, up, down, rows, wv, wc, wr, rm, acc, hid, hsb, prs, kmask, sc, etp_in, pln_in, zout, zin,
+    nb_s, nb_r, x_s, x_r, z_s, z_r, p_s, p_r, l_s, y_s, y_r, s_s, s_r,
     r1_s, r1_r, r2_s, r2_r, r3_s, r3_r, w_sem, hid_sem,
 ):
     e = lax.axis_index("expert")
@@ -131,14 +134,16 @@
         return eqs, any_k, rank == sub_rank
 
     ids_f = ids_ref[...].astype(F32)
-    diff = iota((QUARTER, HALF), 0) - iota((QUARTER, HALF), 1)
+    diff = iota((QUARTER, LATE), 0) - iota((QUARTER, LATE), 1)
     zb0[0, 0:128, :] = dot(og_ref[...], onehot(diff == 48 * q), 0, 0).astype(BF)
     zb0[0, 128:144, 0:128] = jnp.concatenate([ids_f, jnp.zeros((12, 128), F32)], axis=0).astype(BF)
-    zb0[0, 128:144, 128:HALF] = jnp.zeros((16, HALF - 128), BF)
+    zb0[0, 128:144, 128:LATE] = jnp.zeros((16, LATE - 128), BF)
     pl.semaphore_wait(barrier, len(peers))
 
+    zbs, sbs = (zb0, zb1, zb2), (sb0, sb1, sb2)
+
     def zsend(src, i, h, d):
-        buf = zb1 if h else zb0
+        buf = zbs[h]
         send(buf.at[src], buf.at[i], z_s.at[i, h], z_r.at[i, h], zdev(d % PLANES))
 
     send(og_ref.at[pl.ds(0, 144), :], nb, nb_s, nb_r, (e, (q + 3) % 4))
@@ -161,68 +166,78 @@
         return out
 
     def step_second():
-        chunk = dot(og_ref[...], onehot(diff == 48 * q + HALF), 0, 0)
+        diff = iota((QUARTER, EARLY), 0) - iota((QUARTER, EARLY), 1)
+        chunk = dot(og_ref[...], onehot(diff == 48 * q + LATE), 0, 0)
         last = jnp.where(q == 3, 1.0, 0.0)
         tile = last * meta(64)
         arrived(nb, nb_r)
-        gap = jnp.where(q < 3, 48 * q - QUARTER + HALF, 100000)
+        gap = jnp.where(q < 3, 48 * q - QUARTER + LATE, 100000)
         chunk = chunk + dot(nb[...], onehot(diff[:144] == gap), 0, 0)
-        zb1[0] = chunk.astype(BF)
-        zb1[0, :, 128:256] = (chunk[:, 128:256] + tile).astype(BF)
+        zb1[0] = jnp.concatenate([chunk[:, 0:128] + tile, chunk[:, 128:256]], axis=1).astype(BF)
+        send(zb1.at[0], zb2.at[0], x_s, x_r, (e, q2))
         zsend(0, 1, 1, 1)
         zsend(0, 2, 1, -1)
 
     def lanes_of(qq, h):
-        return pl.ds(pl.multiple_of(qq * CHUNK + h * HALF, 128), HALF)
+        if h == 0:
+            return pl.ds(pl.multiple_of(qq * CHUNK, 128), LATE)
+        return pl.ds(pl.multiple_of(qq * CHUNK + LATE, 128), EARLY)
 
     def step_a(i, h):
-        buf = zb1 if h else zb0
+        buf, out = zbs[h], sbs[h]
         if i == 0 and h == 1:
             step_second()
+        if i == 0 and h == 2:
+            arrived(zb2.at[0], x_r)
+            zsend(0, 1, 2, 1)
+            zsend(0, 2, 2, -1)
         if i > 0:
             arrived(buf.at[i], z_r.at[i, h])
-            if i in (1, 3) or (i, h) == (5, 0):
+            if i in (1, 3) or (i == 5 and h == 0):
                 zsend(i, i + 2, h, 1)
             if i in (2, 4):
                 zsend(i, i + 2, h, -1)
-            if (i, h) == (6, 1):
+            if i == 6 and h > 0:
                 zsend(i, 7, h, -1)
         if h == 0:
             _, any_k, hit = routes(zb0[i, 128:144, 0:128].astype(F32), z)
             dsel[i] = onehot(any_k & hit)
         picked = dot(dsel[i], buf[i, 0:128, :], 1, 0)
-        selb[i, h] = picked.astype(BF).reshape(COLS, 2, SLOT, HALF)
+        out[i] = picked.astype(BF).reshape(COLS, 2, SLOT, LATE if h == 0 else EARLY)
+        lanes = lanes_of(q2 if h == 2 else q, h)
         for dx, dy in rels:
             xt = (x + dx) % COLS
             yt = yh if dy == 0 else 1 - yh
             at = dy * COLS + dx
-            send(selb.at[i, h, xt, yt], rows.at[i, x, yh, :, lanes_of(q, h)],
+            send(out.at[i, xt, yt], rows.at[i, x, yh, :, lanes],
                  p_s.at[i, h, at], p_r.at[i, h, at], plane_to(dx, dy))
         pltpu.make_async_copy(
-            selb.at[i, h, x, yh], rows.at[i, x, yh, :, lanes_of(q, h)], l_s.at[i, h]).start()
-
-    def half(i, y, qq, h):
+            out.at[i, x, yh], rows.at[i, x, yh, :, lanes], l_s.at[i, h]).start()
+
+    def part(i, y, qq, h):
         return rows.at[i, :, y, :, lanes_of(qq, h)]
 
     def step_c(i, h):
-        arrived(selb.at[i, h, 0, 0], l_s.at[i, h])
+        arrived(sbs[h].at[i, 0, 0], l_s.at[i, h])
+        qa, qb = (q2, q) if h == 2 else (q, q2)
         for dx, dy in rels:
             xs = (x - dx + COLS) % COLS
             ys = yh if dy == 0 else 1 - yh
-            qs = q if dy == 0 else q2
+            qs = qa if dy == 0 else qb
             arrived(rows.at[i, xs, ys, :, lanes_of(qs, h)], p_r.at[i, h, dy * COLS + dx])
-        one, two = half(i, yh, q, h), half(i, 1 - yh, q2, h)
-        send(one, one, y_s.at[i, h, 0], y_r.at[i, h, 0], (e, q2))
-        send(two, two, y_s.at[i, h, 1], y_r.at[i, h, 1], (e, q2))
+        one, two = part(i, yh, qa, h), part(i, 1 - yh, qb, h)
+        if h == 0:
+            send(one, one, y_s.at[i, 0], y_r.at[i, 0], (e, q2))
+            send(two, two, y_s.at[i, 1], y_r.at[i, 1], (e, q2))
         send(one, one, s_s.at[i, h, 0], s_r.at[i, h, 0], (e, q1))
         send(two, two, s_s.at[i, h, 1], s_r.at[i, h, 1], (e, q1))
 
-    def step_d(i, h):
-        one, two = half(i, yh, q2, h), half(i, 1 - yh, q, h)
-        arrived(one, y_r.at[i, h, 0])
-        send(one, one, s_s.at[i, h, 2], s_r.at[i, h, 2], (e, q1))
-        arrived(two, y_r.at[i, h, 1])
-        send(two, two, s_s.at[i, h, 3], s_r.at[i, h, 3], (e, q1))
+    def step_d(i):
+        one, two = part(i, yh, q2, 0), part(i, 1 - yh, q, 0)
+        arrived(one, y_r.at[i, 0])
+        send(one, one, s_s.at[i, 0, 2], s_r.at[i, 0, 2], (e, q1))
+        arrived(two, y_r.at[i, 1])
+        send(two, two, s_s.at[i, 0, 3], s_r.at[i, 0, 3], (e, q1))
 
     def tables():
         f, c = iota((512, 512), 0), iota((512, 512), 1)
@@ -257,56 +272,54 @@
         for k in range(TOP):
             kmask[i, k] = jnp.where(eqs[k] & hit, 1.0, 0.0)
 
-    def step_g(g):
+    def r(g, lo, n):
+        return rows[2 * g:2 * g + 2, :, :, :, lo:lo + n].reshape(256, n)
+
+    def span(g):
+        return slice(256 * g, 256 * g + 256)
+
+    def step_b(g):
         for i in (2 * g, 2 * g + 1):
-            for h in range(2):
-                arrived(half(i, yh, q1, h), s_r.at[i, h, 0])
-                arrived(half(i, 1 - yh, q3, h), s_r.at[i, h, 1])
-                arrived(half(i, yh, q3, h), s_r.at[i, h, 2])
-                arrived(half(i, 1 - yh, q1, h), s_r.at[i, h, 3])
+            arrived(part(i, yh, q1, 0), s_r.at[i, 0, 0])
+            arrived(part(i, 1 - yh, q3, 0), s_r.at[i, 0, 1])
+            arrived(part(i, yh, q3, 0), s_r.at[i, 0, 2])
+            arrived(part(i, 1 - yh, q1, 0), s_r.at[i, 0, 3])
+            arrived(part(i, yh, q1, 1), s_r.at[i, 1, 0])
+            arrived(part(i, 1 - yh, q3, 1), s_r.at[i, 1, 1])
+            arrived(part(i, yh, q3, 2), s_r.at[i, 2, 0])
+            arrived(part(i, 1 - yh, q1, 2), s_r.at[i, 2, 1])
             hid_cp[i].wait()
-        span = pl.ds(256 * g, 256)
-
-        def r(lo, n):
-            return rows[2 * g:2 * g + 2, :, :, :, lo:lo + n].reshape(256, n)
-
-        back = dot(wr[...], r(0, WIDTH), 1, 1)
-        score = jnp.sum(hid[:, span].astype(F32) * back, axis=0, keepdims=True)
+        back = dot(wr[...], r(g, 0, WIDTH), 1, 1)
+        score = jnp.sum(hid[:, span(g)].astype(F32) * back, axis=0, keepdims=True)
         sc[2 * g:2 * g + 1, :] = score[:, :128]
         sc[2 * g + 1:2 * g + 2, :] = score[:, 128:]
-        if g == 3:
-            return_one()
-        mt = r(META, 128).astype(F32)
+
+    def step_w(g):
+        mt = r(g, META, 128).astype(F32)
         total = pltpu.roll(mt, 124, 1) + pltpu.roll(mt, 120, 1) + pltpu.roll(mt, 116, 1)
         wide = iota((256, 128), 1)
         mine = (wide >= 64) & (wide < 68) & (mt == e.astype(F32))
         pc = jnp.sum(jnp.where(mine, total, 0.0), axis=1, keepdims=True)
         pr = jnp.concatenate([as_row(pc[:128]), as_row(pc[128:])], axis=1)
-        grad = (dot(wc[...], r(0, WIDTH), 1, 1) * pr).astype(BF)
+        prs[:, span(g)] = pr
+        hsb[:, span(g)] = (hid[:, span(g)].astype(F32) * pr).astype(BF)
+        for c in range(4):
+            n = min(CHUNK, WIDTH - CHUNK * c)
+            ln = slice(CHUNK * c, CHUNK * c + n)
+            share = dot(hsb[:, span(g)], r(g, CHUNK * c, n), 1, 0)
+            if g > 0:
+                share = share + acc[:, ln]
+            if g < 3:
+                acc[:, ln] = share
+            else:
+                wg_ref[:, ln] = jnp.where(rm[:, ln].astype(F32) > 0.5, share, 0.0).astype(BF)
+
+    def step_h(g):
+        grad = (dot(wc[...], r(g, 0, WIDTH), 1, 1) * prs[:, span(g)]).astype(BF)
         for i in (2 * g, 2 * g + 1):
             src = (z + rel(i) + PLANES) % PLANES
-            part = 128 * (i % 2)
-            hg_ref[:, pl.ds(pl.multiple_of(src * 128, 128), 128)] = grad[:, part:part + 128]
-        hsb[...] = (hid[:, span].astype(F32) * pr).astype(BF)
-        if g == 3:
-            return_two()
-        if g < 3:
-            for c in range(4):
-                n = min(CHUNK, WIDTH - CHUNK * c)
-                part = dot(hsb[...], r(CHUNK * c, n), 1, 0)
-                if g > 0:
-                    part = part + acc[:, CHUNK * c:CHUNK * c + n]
-                acc[:, CHUNK * c:CHUNK * c + n] = part
-        else:
-            for m in range(3):
-                at = slice(240 * m, 240 * m + 240)
-                for c in range(4):
-                    n = min(CHUNK, WIDTH - CHUNK * c)
-                    ln = slice(CHUNK * c, CHUNK * c + n)
-                    part = dot(hsb[at, :], r(CHUNK * c, n), 1, 0) + acc[at, ln]
-                    wg_ref[at, ln] = jnp.where(rm[at, ln].astype(F32) > 0.5, part, 0.0).astype(BF)
-                if m == 0:
-                    return_three()
+            at = 128 * (i % 2)
+            hg_ref[:, pl.ds(pl.multiple_of(src * 128, 128), 128)] = grad[:, at:at + 128]
 
     def return_one():
         etp_in[q] = sc[...]
@@ -347,10 +360,10 @@
         for k in range(TOP):
             pg_ref[k:k + 1, :] = jnp.sum(totals[k], axis=0, keepdims=True)
 
-    steps = {"A": step_a, "C": step_c, "D": step_d, "M": step_m, "K": step_k, "G": step_g}
+    steps = {"A": step_a, "C": step_c, "D": step_d, "M": step_m, "K": step_k, "B": step_b, "W": step_w, "H": step_h,
+             "R": lambda n: (return_one, return_two, return_three, return_four)[n - 1]()}
     for item in SCHEDULE:
         steps[item[0]](*[int(c) for c in item[1:]])
-    return_four()
     for cp in pending:
         cp.wait_send()
 
@@ -371,9 +384,12 @@
         out_specs=(out, out, vmem),
         scratch_shapes=[
             pltpu.VMEM((144, TOKENS), BF),
-            pltpu.VMEM((8, TOKENS + 16, HALF), BF),
-            pltpu.VMEM((8, TOKENS, HALF), BF),
-            pltpu.VMEM((8, 2, COLS, 2, SLOT, HALF), BF),
+            pltpu.VMEM((8, TOKENS + 16, LATE), BF),
+            pltpu.VMEM((8, TOKENS, EARLY), BF),
+            pltpu.VMEM((8, TOKENS, EARLY), BF),
+            pltpu.VMEM((8, COLS, 2, SLOT, LATE), BF),
+            pltpu.VMEM((8, COLS, 2, SLOT, EARLY), BF),
+            pltpu.VMEM((8, COLS, 2, SLOT, EARLY), BF),
             pltpu.VMEM((8, 128, 128), BF),
             pltpu.VMEM((512, 512), BF),
             pltpu.VMEM((512, 512), BF),
@@ -386,15 +402,16 @@
             pltpu.VMEM((QUARTER, WIDTH), BF),
             pltpu.VMEM((QUARTER, WIDTH), F32),
             pltpu.VMEM((QUARTER, 1024), BF),
-                pltpu.VMEM((QUARTER, 256), BF),
+                pltpu.VMEM((QUARTER, 1024), BF),
+            pltpu.VMEM((1, 1024), F32),
             pltpu.VMEM((8, TOP, 128, 128), F32),
             pltpu.VMEM((8, 128), F32),
             pltpu.VMEM((4, 8, 128), F32),
             pltpu.VMEM((8, 8, 128), F32),
             pltpu.VMEM((8, 128), F32),
             pltpu.VMEM((8, 8, 128), F32),
-            dma, dma, dma((8, 2)), dma((8, 2)), dma((8, 2, 8)), dma((8, 2, 8)), dma((8, 2)),
-            dma((8, 2, 2)), dma((8, 2, 2)), dma((8, 2, 4)), dma((8, 2, 4)),
+            dma, dma, dma, dma, dma((8, 3)), dma((8, 3)), dma((8, 3, 8)), dma((8, 3, 8)), dma((8, 3)),
+            dma((8, 2)), dma((8, 2)), dma((8, 3, 4)), dma((8, 3, 4)),
             dma((4,)), dma((4,)), dma((8,)), dma((8,)), dma((8,)), dma((8,)),
             dma, dma((8,)),
         ],

time: 80.7 us -> 84.7 us (1.050)
  Pallas kernels: 76.3 us -> 80.2 us
    pallas_call x1, Pallas kernels: 76.3 us -> 80.2 us  [call(): pl.pallas_call(kernel, out_shape=(pltpu.VMEM((QUARTER, WIDTH), BF), pltpu...]
where the time goes in v1:
time: 84.7 us; the launch traced here: 84.6 us
  Pallas kernels  80.2 us (95%)
  local copies, waits for them, and re-layouts  3.72 us (4%)
    pallas_call x1, Pallas kernels, call(): pl.pallas_call(kernel, out_shape=(pltpu.VMEM((QUARTER, WIDTH), BF), pltpu...  80.2 us
    unnamed x5, local copies, waits for them, and re-layouts  3.72 us

profile of v1, /device:TPU:1, one launch (start us, length us, event | category | flops | bytes accessed | tf_op | source)
XLA Modules:
  0.0 84.6 jit_solution(7653641480073574029)
XLA Ops:
  0.6 80.2 %shard_map.76 = (bf16[720,2880]{1,0:T(8,128)(2,1)S(1)}, bf16[720,1024]{1,0:T(8,128)(2,1)S(1)}, f32[4,128]{1,0:T(4,128)}) custom-call(s32[4,128]{1,0:T(4,128)} %bitcast.18, f32[4,128]{1,0:T(4,128)} %bitcast.19, bf16[720,128]{1,0:T(8,128)(2,1)} %bitcast.17, bf16[720,2880]{1,0:T(8,128)(2,1)} %bitcast.15, bf16[720,1024]{1,0:T(8,128)(2,1)} %bitcast.16), custom_call_target="tpu_custom_call" | custom-call | flops 12740198400 | bytes 20000000 | tf_op jit(solution)/shard_map/pallas_call | solution.py:376
  80.9 0.0 copy-start
  80.9 2.0 %copy.11 = bf16[1,720,2880]{2,1,0:T(8,128)(2,1)} copy(bf16[1,720,2880]{2,1,0:T(8,128)(2,1)S(1)} %bitcast.12) | data formatting | bytes 8294400
  82.9 1.1 %copy.12 = bf16[1,1024,720]{1,2,0:T(8,128)(2,1)} copy(bf16[1,1024,720]{1,2,0:T(8,128)(2,1)S(1)} %bitcast.13) | data formatting | bytes 2949120
  84.0 0.0 copy-done
  84.0 0.6 copy.13
Async XLA Ops:
  80.9 3.2 %copy-start = (f32[4,128]{1,0:T(4,128)S(1)}, f32[4,128]{1,0:T(4,128)}, u32[]{:S(2)}) copy-start(f32[4,128]{1,0:T(4,128)} %get-tuple-element.8) | copy-start | bytes 6148

commit v2 on v1

--- a/solution.py
+++ b/solution.py
@@ -16,21 +16,19 @@
 CHUNK = 768
 LATE = 512
 EARLY = 256
-META = 2 * CHUNK + 2 * CHUNK - 256
+META = 512
 SLOT = 16
 PLANES = 8
 COLS = 4
 PLANE = 8
 
 SCHEDULE = (
-    "A00", "M0", "A01", "A02", "C00", "A10", "A20", "M1", "C01", "C02", "A11", "A21",
-    "A12", "A22", "C10", "C20", "M2", "A30", "A40", "C11", "C21", "C12", "C22", "A31",
-    "A41", "A32", "A42", "D0", "M3", "C30", "C40", "A50", "A60", "C31", "C41", "C32",
-    "C42", "A51", "A61", "A52", "A62", "D1", "M4", "C50", "C60", "A70", "A71", "A72",
-    "C51", "C61", "C52", "C62", "M5", "C70", "C71", "C72", "D2", "K0", "K1", "K2",
-    "K3", "B0", "W0", "D3", "D4", "B1", "W1", "K4", "K5", "K6", "K7", "D5",
-    "D6", "B2", "D7", "B3", "R1", "W2", "H1", "R2", "W3", "H2", "R3", "H3",
-    "H0", "R4",
+    "T0", "K0", "K1", "K2", "K3", "K4", "K5", "K6", "K7", "N0", "S0", "A0", "E0", "Z1", "Z2", "A1",
+    "A2", "C0", "Y1", "Y2", "E1", "E2", "F0", "N1", "Z3", "Z4", "A3", "A4", "C1", "C2", "N2", "Y3",
+    "Y4", "E3", "E4", "F1", "F2", "Z5", "Z6", "A5", "A6", "C3", "C4", "N3", "Y5", "Y6", "E5", "E6",
+    "D0", "F3", "F4", "Z7", "A7", "C5", "C6", "N4", "Y7", "E7", "D1", "F5", "F6", "N5", "C7", "F7",
+    "D2", "B0", "W0", "D3", "D4", "B1", "W1", "D5", "M0", "M1", "D6", "B2", "D7", "B3", "R1", "W2",
+    "M2", "R2", "W3", "M3", "M4", "M5", "R3", "H0", "H1", "H2", "H3", "R4",
 )
 
 
@@ -47,22 +45,26 @@
 
 
 def keep(a0, a1, a2, a3):
-    b01, b02, b03 = a0 >= a1, a0 >= a2, a0 >= a3
-    b12, b13, b23 = a1 >= a2, a1 >= a3, a2 >= a3
-    n01, n02, n03 = ~b01, ~b02, ~b03
-    n12, n13, n23 = ~b12, ~b13, ~b23
+    one, zero = jnp.ones((), BF), jnp.zeros((), BF)
+
+    def wins(a, b):
+        return jnp.where(a >= b, one, zero)
 
     def two(a, b, c):
-        return onehot((a & b) | (c & (a | b)))
-
-    return two(b01, b02, b03), two(n01, b12, b13), two(n02, n12, b23), two(n03, n13, n23)
+        return jnp.maximum(jnp.minimum(a, b), jnp.minimum(c, jnp.maximum(a, b)))
+
+    w01, w02, w03 = wins(a0, a1), wins(a0, a2), wins(a0, a3)
+    w12, w13, w23 = wins(a1, a2), wins(a1, a3), wins(a2, a3)
+    return (
+        two(w01, w02, w03), two(one - w01, w12, w13),
+        two(one - w02, one - w12, w23), two(one - w03, one - w13, one - w23))
 
 
 def kernel(
     ids_ref, probs_ref, og_ref, w_hbm, hid_hbm,
     wg_ref, hg_ref, pg_ref,
-    nb, zb0, zb1, zb2, sb0, sb1, sb2, dsel, fwd, bwd, up, down, rows, wv, wc, wr, rm, acc, hid, hsb, prs, kmask, sc, etp_in, pln_in, zout, zin,
-    nb_s, nb_r, x_s, x_r, z_s, z_r, p_s, p_r, l_s, y_s, y_r, s_s, s_r,
+    nb, zb0, zb1, sb0, sb1, dsel, fwd, bwd, up, down, rows, wv, wc, wr, rm, acc, hid, hsb, prs, kmask, sc, etp_in, pln_in, zout, zin,
+    nb_s, nb_r, x_s, x_r, z_s, z_r, p_s, p_r, y_s, y_r, s_s, s_r,
     r1_s, r1_r, r2_s, r2_r, r3_s, r3_r, w_sem, hid_sem,
 ):
     e = lax.axis_index("expert")
@@ -73,7 +75,6 @@
     ylo, core = q // 2, q % 2
     q1 = ylo * 2 + 1 - core
     q2 = (1 - ylo) * 2 + core
-    q3 = (1 - ylo) * 2 + 1 - core
     pending = []
 
     def send(src, dst, ss, rs, dev):
@@ -138,17 +139,18 @@
     zb0[0, 0:128, :] = dot(og_ref[...], onehot(diff == 48 * q), 0, 0).astype(BF)
     zb0[0, 128:144, 0:128] = jnp.concatenate([ids_f, jnp.zeros((12, 128), F32)], axis=0).astype(BF)
     zb0[0, 128:144, 128:LATE] = jnp.zeros((16, LATE - 128), BF)
-    pl.semaphore_wait(barrier, len(peers))
-
-    zbs, sbs = (zb0, zb1, zb2), (sb0, sb1, sb2)
+
+    zbs = (zb0, zb1)
 
     def zsend(src, i, h, d):
         buf = zbs[h]
         send(buf.at[src], buf.at[i], z_s.at[i, h], z_r.at[i, h], zdev(d % PLANES))
 
-    send(og_ref.at[pl.ds(0, 144), :], nb, nb_s, nb_r, (e, (q + 3) % 4))
-    zsend(0, 1, 0, 1)
-    zsend(0, 2, 0, -1)
+    def step_s(_):
+        pl.semaphore_wait(barrier, len(peers))
+        send(og_ref.at[pl.ds(0, 144), :], nb, nb_s, nb_r, (e, (q + 3) % 4))
+        zsend(0, 1, 0, 1)
+        zsend(0, 2, 0, -1)
 
     probs = probs_ref[...]
     own_ids = [column(ids_f[k:k + 1, :]) for k in range(TOP)]
@@ -173,73 +175,74 @@
         arrived(nb, nb_r)
         gap = jnp.where(q < 3, 48 * q - QUARTER + LATE, 100000)
         chunk = chunk + dot(nb[...], onehot(diff[:144] == gap), 0, 0)
-        zb1[0] = jnp.concatenate([chunk[:, 0:128] + tile, chunk[:, 128:256]], axis=1).astype(BF)
-        send(zb1.at[0], zb2.at[0], x_s, x_r, (e, q2))
-        zsend(0, 1, 1, 1)
-        zsend(0, 2, 1, -1)
-
-    def lanes_of(qq, h):
-        if h == 0:
-            return pl.ds(pl.multiple_of(qq * CHUNK, 128), LATE)
-        return pl.ds(pl.multiple_of(qq * CHUNK + LATE, 128), EARLY)
-
-    def step_a(i, h):
-        buf, out = zbs[h], sbs[h]
-        if i == 0 and h == 1:
-            step_second()
-        if i == 0 and h == 2:
-            arrived(zb2.at[0], x_r)
-            zsend(0, 1, 2, 1)
-            zsend(0, 2, 2, -1)
-        if i > 0:
-            arrived(buf.at[i], z_r.at[i, h])
-            if i in (1, 3) or (i == 5 and h == 0):
-                zsend(i, i + 2, h, 1)
-            if i in (2, 4):
-                zsend(i, i + 2, h, -1)
-            if i == 6 and h > 0:
-                zsend(i, 7, h, -1)
-        if h == 0:
-            _, any_k, hit = routes(zb0[i, 128:144, 0:128].astype(F32), z)
-            dsel[i] = onehot(any_k & hit)
-        picked = dot(dsel[i], buf[i, 0:128, :], 1, 0)
-        out[i] = picked.astype(BF).reshape(COLS, 2, SLOT, LATE if h == 0 else EARLY)
-        lanes = lanes_of(q2 if h == 2 else q, h)
+        zb1[0, ylo] = jnp.concatenate(
+            [chunk[:, 0:128] + tile, chunk[:, 128:256]], axis=1).astype(BF)
+        send(zb1.at[0, ylo], zb1.at[0, ylo], x_s, x_r, (e, q2))
+
+    late, early = pl.ds(0, LATE), pl.ds(LATE, EARLY)
+
+    def come(i, h):
+        arrived(zbs[h].at[i], z_r.at[i, h])
+        if i in (1, 3) or (i == 5 and h == 0):
+            zsend(i, i + 2, h, 1)
+        if i in (2, 4):
+            zsend(i, i + 2, h, -1)
+        if i == 6 and h == 1:
+            zsend(i, 7, h, -1)
+
+    def to_plane(i, h, src, dst, sems):
         for dx, dy in rels:
             xt = (x + dx) % COLS
             yt = yh if dy == 0 else 1 - yh
-            at = dy * COLS + dx
-            send(out.at[i, xt, yt], rows.at[i, x, yh, :, lanes],
-                 p_s.at[i, h, at], p_r.at[i, h, at], plane_to(dx, dy))
-        pltpu.make_async_copy(
-            out.at[i, x, yh], rows.at[i, x, yh, :, lanes], l_s.at[i, h]).start()
-
-    def part(i, y, qq, h):
-        return rows.at[i, :, y, :, lanes_of(qq, h)]
-
-    def step_c(i, h):
-        arrived(sbs[h].at[i, 0, 0], l_s.at[i, h])
-        qa, qb = (q2, q) if h == 2 else (q, q2)
-        for dx, dy in rels:
-            xs = (x - dx + COLS) % COLS
-            ys = yh if dy == 0 else 1 - yh
-            qs = qa if dy == 0 else qb
-            arrived(rows.at[i, xs, ys, :, lanes_of(qs, h)], p_r.at[i, h, dy * COLS + dx])
-        one, two = part(i, yh, qa, h), part(i, 1 - yh, qb, h)
-        if h == 0:
-            send(one, one, y_s.at[i, 0], y_r.at[i, 0], (e, q2))
-            send(two, two, y_s.at[i, 1], y_r.at[i, 1], (e, q2))
-        send(one, one, s_s.at[i, h, 0], s_r.at[i, h, 0], (e, q1))
-        send(two, two, s_s.at[i, h, 1], s_r.at[i, h, 1], (e, q1))
+            send(src.at[i, xt, yt], dst, p_s.at[i, h, dy * COLS + dx], sems[dy], plane_to(dx, dy))
+        pltpu.make_async_copy(src.at[i, x, yh], dst, sems[0]).start()
+
+    def step_a(i):
+        _, any_k, hit = routes(zb0[i, 128:144, 0:128].astype(F32), z)
+        dsel[i] = onehot(any_k & hit)
+        picked = dot(dsel[i], zb0[i, 0:128, :], 1, 0)
+        sb0[i] = picked.astype(BF).reshape(COLS, 2, SLOT, LATE)
+        to_plane(i, 0, sb0, rows.at[i, x, yh, ylo, core, :, late], (p_r.at[i, 0], p_r.at[i, 1]))
+        if i == 0:
+            step_second()
+
+    def step_e(i):
+        if i == 0:
+            arrived(zb1.at[0, 1 - ylo], x_r)
+            zsend(0, 1, 1, 1)
+            zsend(0, 2, 1, -1)
+        for y in range(2):
+            picked = dot(dsel[i], zb1[i, y], 1, 0)
+            sb1[i, :, :, y] = picked.astype(BF).reshape(COLS, 2, SLOT, EARLY)
+        to_plane(i, 1, sb1, rows.at[i, x, yh, :, core, :, early], (p_r.at[i, 2], p_r.at[i, 2]))
+
+    def part(i, y, yl, c):
+        return rows.at[i, :, y, yl, c, :, late]
+
+    def both(i, c):
+        return rows.at[i, :, :, :, c, :, early]
+
+    def step_c(i):
+        one, two = part(i, yh, ylo, core), part(i, 1 - yh, 1 - ylo, core)
+        arrived(one, p_r.at[i, 0])
+        send(one, one, y_s.at[i, 0], y_r.at[i, 0], (e, q2))
+        arrived(two, p_r.at[i, 1])
+        send(two, two, y_s.at[i, 1], y_r.at[i, 1], (e, q2))
+        send(one, one, s_s.at[i, 0], s_r.at[i, 0], (e, q1))
+        send(two, two, s_s.at[i, 1], s_r.at[i, 1], (e, q1))
+
+    def step_f(i):
+        arrived(both(i, core), p_r.at[i, 2])
+        send(both(i, core), both(i, core), s_s.at[i, 4], s_r.at[i, 4], (e, q1))
 
     def step_d(i):
-        one, two = part(i, yh, q2, 0), part(i, 1 - yh, q, 0)
+        one, two = part(i, yh, 1 - ylo, core), part(i, 1 - yh, ylo, core)
         arrived(one, y_r.at[i, 0])
-        send(one, one, s_s.at[i, 0, 2], s_r.at[i, 0, 2], (e, q1))
+        send(one, one, s_s.at[i, 2], s_r.at[i, 2], (e, q1))
         arrived(two, y_r.at[i, 1])
-        send(two, two, s_s.at[i, 0, 3], s_r.at[i, 0, 3], (e, q1))
-
-    def tables():
+        send(two, two, s_s.at[i, 3], s_r.at[i, 3], (e, q1))
+
+    def tables(_):
         f, c = iota((512, 512), 0), iota((512, 512), 1)
         fwd[...] = onehot((c % 128 == f // 4) & (c // 128 == f % 4))
         c, f = iota((512, 512), 0), iota((512, 512), 1)
@@ -248,54 +251,58 @@
         up[...] = onehot((c % 64 == f // 4) & (c // 64 == f % 4))
         f, c = iota((240, 256), 0), iota((240, 256), 1)
         down[...] = onehot((c % 64 == f // 4) & (c // 64 == f % 4))
+        w_cp.wait()
 
     def step_m(b):
-        if b == 0:
-            tables()
-            w_cp.wait()
         lo = 512 * b
         n = min(512, WIDTH - lo)
         wb = wv[:, lo:lo + n]
         a = jnp.abs(dot(wb, fwd[0:n, :], 1, 0)).astype(BF)
         kept = jnp.concatenate(keep(*[a[:, 128 * p:128 * p + 128] for p in range(4)]), axis=1)
         wc[:, lo:lo + n] = wb * dot(kept, bwd[:, 0:n], 1, 0).astype(BF)
+
+    def step_n(b):
+        lo = 512 * b
+        n = min(512, WIDTH - lo)
         for m in range(3):
-            part = wb[240 * m:240 * m + 240]
-            a = jnp.abs(dot(up[...], part, 1, 0)).astype(BF)
+            at = slice(240 * m, 240 * m + 240)
+            wb = wv[at, lo:lo + n]
+            a = jnp.abs(dot(up[...], wb, 1, 0)).astype(BF)
             kept = jnp.concatenate(keep(*[a[64 * p:64 * p + 64] for p in range(4)]), axis=0)
             mask = dot(down[...], kept, 1, 0).astype(BF)
-            rm[240 * m:240 * m + 240, lo:lo + n] = mask
-            wr[240 * m:240 * m + 240, lo:lo + n] = part * mask
+            rm[at, lo:lo + n] = mask
+            wr[at, lo:lo + n] = wb * mask
 
     def step_k(i):
         eqs, _, hit = routes(ids_f, (z - rel(i) + PLANES) % PLANES)
         for k in range(TOP):
             kmask[i, k] = jnp.where(eqs[k] & hit, 1.0, 0.0)
 
-    def r(g, lo, n):
-        return rows[2 * g:2 * g + 2, :, :, :, lo:lo + n].reshape(256, n)
+    def r(g, qq, lo, n):
+        return rows[2 * g:2 * g + 2, :, :, qq // 2, qq % 2, :, lo:lo + n].reshape(256, n)
+
+    def wide_r(g):
+        return jnp.concatenate(
+            [r(g, c, 0, min(CHUNK, WIDTH - CHUNK * c)) for c in range(4)], axis=1)
 
     def span(g):
         return slice(256 * g, 256 * g + 256)
 
     def step_b(g):
         for i in (2 * g, 2 * g + 1):
-            arrived(part(i, yh, q1, 0), s_r.at[i, 0, 0])
-            arrived(part(i, 1 - yh, q3, 0), s_r.at[i, 0, 1])
-            arrived(part(i, yh, q3, 0), s_r.at[i, 0, 2])
-            arrived(part(i, 1 - yh, q1, 0), s_r.at[i, 0, 3])
-            arrived(part(i, yh, q1, 1), s_r.at[i, 1, 0])
-            arrived(part(i, 1 - yh, q3, 1), s_r.at[i, 1, 1])
-            arrived(part(i, yh, q3, 2), s_r.at[i, 2, 0])
-            arrived(part(i, 1 - yh, q1, 2), s_r.at[i, 2, 1])
+            arrived(part(i, yh, ylo, 1 - core), s_r.at[i, 0])
+            arrived(part(i, 1 - yh, 1 - ylo, 1 - core), s_r.at[i, 1])
+            arrived(part(i, yh, 1 - ylo, 1 - core), s_r.at[i, 2])
+            arrived(part(i, 1 - yh, ylo, 1 - core), s_r.at[i, 3])
+            arrived(both(i, 1 - core), s_r.at[i, 4])
             hid_cp[i].wait()
-        back = dot(wr[...], r(g, 0, WIDTH), 1, 1)
+        back = dot(wr[...], wide_r(g), 1, 1)
         score = jnp.sum(hid[:, span(g)].astype(F32) * back, axis=0, keepdims=True)
         sc[2 * g:2 * g + 1, :] = score[:, :128]
         sc[2 * g + 1:2 * g + 2, :] = score[:, 128:]
 
     def step_w(g):
-        mt = r(g, META, 128).astype(F32)
+        mt = r(g, 3, META, 128).astype(F32)
         total = pltpu.roll(mt, 124, 1) + pltpu.roll(mt, 120, 1) + pltpu.roll(mt, 116, 1)
         wide = iota((256, 128), 1)
         mine = (wide >= 64) & (wide < 68) & (mt == e.astype(F32))
@@ -306,7 +313,7 @@
         for c in range(4):
             n = min(CHUNK, WIDTH - CHUNK * c)
             ln = slice(CHUNK * c, CHUNK * c + n)
-            share = dot(hsb[:, span(g)], r(g, CHUNK * c, n), 1, 0)
+            share = dot(hsb[:, span(g)], r(g, c, 0, n), 1, 0)
             if g > 0:
                 share = share + acc[:, ln]
             if g < 3:
@@ -315,7 +322,7 @@
                 wg_ref[:, ln] = jnp.where(rm[:, ln].astype(F32) > 0.5, share, 0.0).astype(BF)
 
     def step_h(g):
-        grad = (dot(wc[...], r(g, 0, WIDTH), 1, 1) * prs[:, span(g)]).astype(BF)
+        grad = (dot(wc[...], wide_r(g), 1, 1) * prs[:, span(g)]).astype(BF)
         for i in (2 * g, 2 * g + 1):
             src = (z + rel(i) + PLANES) % PLANES
             at = 128 * (i % 2)
@@ -360,10 +367,11 @@
         for k in range(TOP):
             pg_ref[k:k + 1, :] = jnp.sum(totals[k], axis=0, keepdims=True)
 
-    steps = {"A": step_a, "C": step_c, "D": step_d, "M": step_m, "K": step_k, "B": step_b, "W": step_w, "H": step_h,
+    steps = {"A": step_a, "C": step_c, "D": step_d, "E": step_e, "F": step_f, "M": step_m,
+             "N": step_n, "Z": lambda i: come(i, 0), "Y": lambda i: come(i, 1), "T": tables, "S": step_s, "K": step_k, "B": step_b, "W": step_w, "H": step_h,
              "R": lambda n: (return_one, return_two, return_three, return_four)[n - 1]()}
     for item in SCHEDULE:
-        steps[item[0]](*[int(c) for c in item[1:]])
+        steps[item[0]](int(item[1:]))
     for cp in pending:
         cp.wait_send()
 
@@ -385,17 +393,15 @@
         scratch_shapes=[
             pltpu.VMEM((144, TOKENS), BF),
             pltpu.VMEM((8, TOKENS + 16, LATE), BF),
-            pltpu.VMEM((8, TOKENS, EARLY), BF),
-            pltpu.VMEM((8, TOKENS, EARLY), BF),
+            pltpu.VMEM((8, 2, TOKENS, EARLY), BF),
             pltpu.VMEM((8, COLS, 2, SLOT, LATE), BF),
-            pltpu.VMEM((8, COLS, 2, SLOT, EARLY), BF),
-            pltpu.VMEM((8, COLS, 2, SLOT, EARLY), BF),
+            pltpu.VMEM((8, COLS, 2, 2, SLOT, EARLY), BF),
             pltpu.VMEM((8, 128, 128), BF),
             pltpu.VMEM((512, 512), BF),
             pltpu.VMEM((512, 512), BF),
             pltpu.VMEM((256, 240), BF),
             pltpu.VMEM((240, 256), BF),
-            pltpu.VMEM((8, COLS, 2, SLOT, 4 * CHUNK), BF),
+            pltpu.VMEM((8, COLS, 2, 2, 2, SLOT, CHUNK), BF),
             pltpu.VMEM((QUARTER, WIDTH), BF),
             pltpu.VMEM((QUARTER, WIDTH), BF),
             pltpu.VMEM((QUARTER, WIDTH), BF),
@@ -410,8 +416,8 @@
             pltpu.VMEM((8, 8, 128), F32),
             pltpu.VMEM((8, 128), F32),
             pltpu.VMEM((8, 8, 128), F32),
-            dma, dma, dma, dma, dma((8, 3)), dma((8, 3)), dma((8, 3, 8)), dma((8, 3, 8)), dma((8, 3)),
-            dma((8, 2)), dma((8, 2)), dma((8, 3, 4)), dma((8, 3, 4)),
+            dma, dma, dma, dma, dma((8, 2)), dma((8, 2)), dma((8, 2, 8)), dma((8, 3)),
+            dma((8, 2)), dma((8, 2)), dma((8, 5)), dma((8, 5)),
             dma((4,)), dma((4,)), dma((8,)), dma((8,)), dma((8,)), dma((8,)),
             dma, dma((8,)),
         ],

time: 84.7 us -> 80.6 us (0.952)
  Pallas kernels: 80.2 us -> 76.1 us
    pallas_call x1, Pallas kernels: 80.2 us -> 76.1 us  [call(): pl.pallas_call(kernel, out_shape=(pltpu.VMEM((QUARTER, WIDTH), BF), pltpu...]
where the time goes in v2:
time: 80.6 us; the launch traced here: 80.5 us
  Pallas kernels  76.1 us (94%)
  local copies, waits for them, and re-layouts  3.72 us (5%)
    pallas_call x1, Pallas kernels, call(): pl.pallas_call(kernel, out_shape=(pltpu.VMEM((QUARTER, WIDTH), BF), pltpu...  76.1 us
    unnamed x5, local copies, waits for them, and re-layouts  3.72 us

profile of v2, /device:TPU:1, one launch (start us, length us, event | category | flops | bytes accessed | tf_op | source)
XLA Modules:
  0.0 80.5 jit_solution(12514770533432925917)
XLA Ops:
  0.6 76.1 %shard_map.76 = (bf16[720,2880]{1,0:T(8,128)(2,1)S(1)}, bf16[720,1024]{1,0:T(8,128)(2,1)S(1)}, f32[4,128]{1,0:T(4,128)}) custom-call(s32[4,128]{1,0:T(4,128)} %bitcast.18, f32[4,128]{1,0:T(4,128)} %bitcast.19, bf16[720,128]{1,0:T(8,128)(2,1)} %bitcast.17, bf16[720,2880]{1,0:T(8,128)(2,1)} %bitcast.15, bf16[720,1024]{1,0:T(8,128)(2,1)} %bitcast.16), custom_call_target="tpu_custom_call" | custom-call | flops 12740198400 | bytes 20000000 | tf_op jit(solution)/shard_map/pallas_call | solution.py:384
  76.7 0.0 copy-start
  76.8 2.0 %copy.11 = bf16[1,720,2880]{2,1,0:T(8,128)(2,1)} copy(bf16[1,720,2880]{2,1,0:T(8,128)(2,1)S(1)} %bitcast.12) | data formatting | bytes 8294400
  78.8 1.1 %copy.12 = bf16[1,1024,720]{1,2,0:T(8,128)(2,1)} copy(bf16[1,1024,720]{1,2,0:T(8,128)(2,1)S(1)} %bitcast.13) | data formatting | bytes 2949120
  79.9 0.0 copy-done
  79.9 0.6 copy.13
Async XLA Ops:
  76.7 3.2 %copy-start = (f32[4,128]{1,0:T(4,128)S(1)}, f32[4,128]{1,0:T(4,128)}, u32[]{:S(2)}) copy-start(f32[4,128]{1,0:T(4,128)} %get-tuple-element.8) | copy-start | bytes 6148

commit v3 on v2

--- a/solution.py
+++ b/solution.py
@@ -23,10 +23,10 @@
 PLANE = 8
 
 SCHEDULE = (
-    "T0", "K0", "K1", "K2", "K3", "K4", "K5", "K6", "K7", "N0", "S0", "A0", "E0", "Z1", "Z2", "A1",
-    "A2", "C0", "Y1", "Y2", "E1", "E2", "F0", "N1", "Z3", "Z4", "A3", "A4", "C1", "C2", "N2", "Y3",
-    "Y4", "E3", "E4", "F1", "F2", "Z5", "Z6", "A5", "A6", "C3", "C4", "N3", "Y5", "Y6", "E5", "E6",
-    "D0", "F3", "F4", "Z7", "A7", "C5", "C6", "N4", "Y7", "E7", "D1", "F5", "F6", "N5", "C7", "F7",
+    "T0", "K0", "K1", "K2", "K3", "K4", "K5", "K6", "K7", "N0", "N1", "S0", "A0", "N2", "N3", "E0",
+    "Z1", "Z2", "A1", "A2", "Y1", "Y2", "C0", "E1", "E2", "Z3", "Z4", "F0", "A3", "A4", "C1", "C2",
+    "Y3", "Y4", "E3", "E4", "F1", "F2", "Z5", "Z6", "A5", "A6", "C3", "C4", "Y5", "Y6", "E5", "E6",
+    "F3", "F4", "Z7", "A7", "Y7", "E7", "D0", "C5", "C6", "F5", "F6", "N4", "D1", "N5", "C7", "F7",
     "D2", "B0", "W0", "D3", "D4", "B1", "W1", "D5", "M0", "M1", "D6", "B2", "D7", "B3", "R1", "W2",
     "M2", "R2", "W3", "M3", "M4", "M5", "R3", "H0", "H1", "H2", "H3", "R4",
 )

time: 80.6 us -> 81.3 us (level)
  no operation moved by 1% of the time
where the time goes in v3:
time: 81.3 us; the launch traced here: 81.2 us
  Pallas kernels  76.8 us (94%)
  local copies, waits for them, and re-layouts  3.72 us (5%)
    pallas_call x1, Pallas kernels, call(): pl.pallas_call(kernel, out_shape=(pltpu.VMEM((QUARTER, WIDTH), BF), pltpu...  76.8 us
    unnamed x5, local copies, waits for them, and re-layouts  3.72 us

profile of v3, /device:TPU:1, one launch (start us, length us, event | category | flops | bytes accessed | tf_op | source)
XLA Modules:
  0.0 81.2 jit_solution(6543060744939847892)
XLA Ops:
  0.6 76.8 %shard_map.76 = (bf16[720,2880]{1,0:T(8,128)(2,1)S(1)}, bf16[720,1024]{1,0:T(8,128)(2,1)S(1)}, f32[4,128]{1,0:T(4,128)}) custom-call(s32[4,128]{1,0:T(4,128)} %bitcast.18, f32[4,128]{1,0:T(4,128)} %bitcast.19, bf16[720,128]{1,0:T(8,128)(2,1)} %bitcast.17, bf16[720,2880]{1,0:T(8,128)(2,1)} %bitcast.15, bf16[720,1024]{1,0:T(8,128)(2,1)} %bitcast.16), custom_call_target="tpu_custom_call" | custom-call | flops 12740198400 | bytes 20000000 | tf_op jit(solution)/shard_map/pallas_call | solution.py:384
  77.4 0.0 copy-start
  77.5 2.0 %copy.11 = bf16[1,720,2880]{2,1,0:T(8,128)(2,1)} copy(bf16[1,720,2880]{2,1,0:T(8,128)(2,1)S(1)} %bitcast.12) | data formatting | bytes 8294400
  79.5 1.1 %copy.12 = bf16[1,1024,720]{1,2,0:T(8,128)(2,1)} copy(bf16[1,1024,720]{1,2,0:T(8,128)(2,1)S(1)} %bitcast.13) | data formatting | bytes 2949120
  80.6 0.0 copy-done
  80.6 0.6 copy.13
Async XLA Ops:
  77.4 3.2 %copy-start = (f32[4,128]{1,0:T(4,128)S(1)}, f32[4,128]{1,0:T(4,128)}, u32[]{:S(2)}) copy-start(f32[4,128]{1,0:T(4,128)} %get-tuple-element.8) | copy-start | bytes 6148
